TPU v7x, 512 devices: a whole 4x8x8 slice. The times are simulated.
512 devices in a mesh: dp: 16 (over z, y_hi), seq: 8 (over y_lo, core), tensor: 4 (over x).
Axes of the slice: x: 4, y: 8 (y_hi: 2, y_lo: 4; y = y_hi * 4 + y_lo), z: 8, core: 2. Of those that a mesh axis runs over, the one named last changes fastest.
Arguments:
- activations: bfloat16 [32768, 512], P(('dp', 'seq')), may hold values from -6 to 6
- d_logits: bfloat16 [32768, 8192], P(('dp', 'seq'), 'tensor'), may hold values from -0.015625 to 0.015625
- block_owner: int32 [16], replicated, may hold values from 0 to 15, each once
- left_stat: float32 [16, 512, 512], P('dp', ('seq', 'tensor')), may hold values from -0.1 to 2.1
- right_stat: float32 [16, 512, 512], P('dp', ('seq', 'tensor')), may hold values from -0.1 to 2.1
- second_moment: float32 [16, 512, 512], P('dp', ('seq', 'tensor')), may hold values from 2e-05 to 0.002
- left_root: float32 [16, 512, 512], P('dp', ('seq', 'tensor')), may hold values from -0.15 to 14
- right_root: float32 [16, 512, 512], P('dp', ('seq', 'tensor')), may hold values from -0.15 to 14
Outputs:
- update: bfloat16 [16, 512, 512], P(None, ('seq', 'tensor'))
- left_new: float32 [16, 512, 512], P('dp', ('seq', 'tensor'))
- right_new: float32 [16, 512, 512], P('dp', ('seq', 'tensor'))
- moment_new: float32 [16, 512, 512], P('dp', ('seq', 'tensor'))
All inputs are finite; a program needn't handle non-finite values.
Results may differ from a plain program's by a relative error of at most 0.00055.
Values may be sent and summed in bfloat16 or wider, within the bound.
A program may use at most 64 MiB of HBM per device.

v0:
```python
import jax
import jax.numpy as jnp
from jax import lax
from jax.sharding import PartitionSpec as P

highest = lax.Precision.HIGHEST


def gradient_rows(logit_columns, activations):
    return lax.dot_general(
        logit_columns, activations, (((0,), (0,)), ((), ())), preferred_element_type=jnp.float32
    )


def per_device(
    activations, d_logits, block_owner, left_stat, right_stat, second_moment, left_root, right_root
):
    tokens_here = d_logits.shape[0]
    block_count = block_owner.shape[0]
    block_width = activations.shape[1]
    seq_count = lax.axis_size("seq")
    tensor_count = lax.axis_size("tensor")
    row_share = block_width // (seq_count * tensor_count)
    block_band = block_width // tensor_count
    indices = jnp.arange(block_count, dtype=jnp.int32)
    matches = block_owner[None, :] == indices[:, None]
    owner_block = jnp.sum(jnp.where(matches, indices[None, :], 0), axis=1)
    by_owner = jnp.take(d_logits.reshape(tokens_here, block_count, block_band), owner_block, axis=1)
    by_owner = by_owner.reshape(tokens_here, block_count * block_band)
    grad_slab = lax.psum_scatter(
        gradient_rows(by_owner, activations), ("dp", "seq"), scatter_dimension=0, tiled=True
    )
    moment_next = 0.99 * second_moment[0] + 0.01 * grad_slab * grad_slab
    adam_dir = grad_slab / (jnp.sqrt(moment_next) + 1e-08)
    adam_part = jnp.sum(adam_dir * adam_dir)
    adam_total = lax.psum(adam_part, ("seq", "tensor"))
    first_row = (lax.axis_index("seq") * tensor_count + lax.axis_index("tensor")) * row_share
    left_rows = left_root[0]
    slab_rows = lax.all_gather(grad_slab, ("seq", "tensor"), axis=0, tiled=True)
    outer_rows = jnp.dot(
        grad_slab, slab_rows.T, precision=highest, preferred_element_type=jnp.float32
    )
    own_columns = lax.dynamic_slice_in_dim(slab_rows, first_row, row_share, 1)
    right_part = jnp.dot(
        own_columns.T, slab_rows, precision=highest, preferred_element_type=jnp.float32
    )
    mixed_part = jnp.dot(
        left_rows, slab_rows, precision=highest, preferred_element_type=jnp.float32
    )
    left_next = 0.95 * left_stat[0] + outer_rows
    right_next = 0.95 * right_stat[0] + right_part
    precond = jnp.dot(
        mixed_part,
        lax.all_gather(right_root[0], ("seq", "tensor"), axis=0, tiled=True),
        precision=highest,
        preferred_element_type=jnp.float32,
    )
    precond_part = jnp.sum(precond * precond)
    precond_total = lax.psum(precond_part, ("seq", "tensor"))
    graft_scale = jnp.sqrt(adam_total) / (jnp.sqrt(precond_total) + 1e-06)
    update_rows = (graft_scale * precond).astype(jnp.bfloat16)
    gathered = lax.all_gather(update_rows[None], "dp", axis=0, tiled=True)
    update = jnp.take(gathered, block_owner, axis=0)
    return (update, left_next[None], right_next[None], moment_next[None])


def solution(mesh):
    return jax.shard_map(
        per_device,
        mesh=mesh,
        in_specs=(
            P(("dp", "seq"), None),
            P(("dp", "seq"), "tensor"),
            P(),
            P("dp", ("seq", "tensor"), None),
            P("dp", ("seq", "tensor"), None),
            P("dp", ("seq", "tensor"), None),
            P("dp", ("seq", "tensor"), None),
            P("dp", ("seq", "tensor"), None),
        ),
        out_specs=(
            P(None, ("seq", "tensor"), None),
            P("dp", ("seq", "tensor"), None),
            P("dp", ("seq", "tensor"), None),
            P("dp", ("seq", "tensor"), None),
        ),
        check_vma=False,
    )
```

profile of v0, /device:TPU:2, one launch (start us, length us, event | category | flops | bytes accessed | tf_op | source)
XLA Modules:
  0.0 537.0 jit_solution(10897611241762053604)
XLA Ops:
  7.2 0.0 copy-start
  7.2 0.0 reduce-scatter.2.cloned.1.call-start
  7.2 0.8 select_reduce_fusion
  8.1 1.5 copy.15
  9.6 0.7 copy.16
  10.2 0.7 gather_fusion
  11.0 0.5 copy.17
  11.5 0.1 broadcast_bitcast_fusion
  11.6 0.5 bitcast_select_fusion
  12.1 0.0 copy-done
  12.1 2.6 fusion.11
  14.8 0.0 copy-start.6
  14.8 0.0 copy-start.2
  14.8 0.0 copy-start.3
  14.8 0.0 copy-start.4
  14.8 0.0 copy-start.5
  14.8 0.0 reduce-scatter.2.cloned.1.call-update
  14.8 0.0 all-gather.5.cloned.1.call-start
  14.9 206.3 %reduce-scatter.2.cloned.1.call-done = f32[16,512]{1,0:T(8,128)} async-done(((f32[2048,512]{1,0:T(8,128)}), f32[16,512]{1,0:T(8,128)}) %reduce-scatter.2.cloned.1.call-update) | async-done | bytes 32784 | tf_op jit(solution)/shard_map/reduce_scatter | solution.py:30
  221.1 0.0 all-gather.5.cloned.1.call-update
  221.2 0.0 all-gather.7.cloned.1.call-start
  221.2 0.7 all-gather.7.cloned.1.call-update
  221.9 0.0 copy-done.6
  222.0 0.0 copy-done.2
  222.0 2.0 fusion.8
  224.0 83.4 %all-gather.5.cloned.1.call-done = f32[512,512]{1,0:T(8,128)} async-done(((f32[16,512]{1,0:T(8,128)}), f32[512,512]{1,0:T(8,128)}) %all-gather.5.cloned.1.call-update) | async-done | bytes 1048592 | tf_op jit(solution)/shard_map/all_gather | solution.py:39
  307.3 0.0 copy-done.3
  307.3 0.0 copy-start.1
  307.3 2.0 fusion.6
  309.3 87.3 %all-gather.7.cloned.1.call-done = f32[1,512,512]{2,1,0:T(8,128)} async-done(((f32[1,16,512]{2,1,0:T(8,128)}), f32[1,512,512]{2,1,0:T(8,128)}) %all-gather.7.cloned.1.call-update) | async-done | bytes 1048592 | tf_op jit(solution)/shard_map/all_gather | solution.py:54
  396.6 2.4 multiply_reduce_fusion
  399.1 69.5 %all-reduce = (f32[]{:T(128)}, f32[]{:T(128)}) all-reduce(f32[]{:T(128)} %get-tuple-element.7, f32[]{:T(128)} %get-tuple-element.8), channel_id=1, replica_groups=mesh['dp'=16,'seq'=8,'tensor'=4] {'seq','tensor'}, use_global_device_ids=true, to_apply=%region_3.4 | all-reduce | flops 2 | bytes 16 | tf_op jit(solution)/shard_map/psum | solution.py:36
  470.0 55.5 %all-gather.1 = bf16[256,512]{1,0:T(8,128)(2,1)S(1)} all-gather(bf16[16,512]{1,0:T(8,128)(2,1)S(1)} %multiply_convert_fusion), channel_id=3, replica_groups=mesh['dp'=16,'seq'=8,'tensor'=4] {'dp'}, dimensions={0}, use_global_device_ids=true | all-gather | bytes 278528 | tf_op jit(solution)/shard_map/all_gather | solution.py:62
  525.5 0.6 gather_fusion.1
  526.0 0.8 broadcast_select_fusion
  526.8 0.0 copy-done.4
  526.8 0.0 copy-done.1
  526.8 2.3 fusion
  529.2 0.0 copy-done.5
  529.2 1.3 fusion.1
  (7 shorter events, 0.0 us)
Async XLA Ops:
  7.2 5.0 copy-start
  7.2 214.0 %reduce-scatter.2.cloned.1.call-start = ((), (), s32[]{:S(2)}) async-start(), calls=%async_computation.1 | async-start | bytes 4227072 | tf_op jit(solution)/shard_map/reduce_scatter | solution.py:30
  14.8 207.1 %copy-start.6 = (s32[16]{0:T(128)S(1)}, s32[16]{0:T(128)}, u32[]{:S(2)}) copy-start(s32[16]{0:T(128)} %param.10) | copy-start | bytes 196
  14.8 207.2 %copy-start.2 = (f32[1,16,512]{2,1,0:T(8,128)S(1)}, f32[1,16,512]{2,1,0:T(8,128)}, u32[]{:S(2)}) copy-start(f32[1,16,512]{2,1,0:T(8,128)} %param.13) | copy-start | bytes 98308
  14.8 292.6 %copy-start.3 = (f32[1,16,512]{2,1,0:T(8,128)S(1)}, f32[1,16,512]{2,1,0:T(8,128)}, u32[]{:S(2)}) copy-start(f32[1,16,512]{2,1,0:T(8,128)} %param.14) | copy-start | bytes 98308
  14.8 512.1 %copy-start.4 = (f32[1,16,512]{2,1,0:T(8,128)S(1)}, f32[1,16,512]{2,1,0:T(8,128)}, u32[]{:S(2)}) copy-start(f32[1,16,512]{2,1,0:T(8,128)} %param.11) | copy-start | bytes 98308
  14.8 514.4 %copy-start.5 = (f32[1,16,512]{2,1,0:T(8,128)S(1)}, f32[1,16,512]{2,1,0:T(8,128)}, u32[]{:S(2)}) copy-start(f32[1,16,512]{2,1,0:T(8,128)} %param.12) | copy-start | bytes 98308
  14.8 292.5 %all-gather.5.cloned.1.call-start = ((), (), s32[]{:S(2)}) async-start(), calls=%async_computation.2 | async-start | bytes 1081344 | tf_op jit(solution)/shard_map/all_gather | solution.py:39
  221.2 175.4 %all-gather.7.cloned.1.call-start = ((), (), s32[]{:S(2)}) async-start(), calls=%async_computation.3 | async-start | bytes 1081344 | tf_op jit(solution)/shard_map/all_gather | solution.py:54
  307.3 219.5 %copy-start.1 = (f32[512,512]{1,0:T(8,128)S(1)}, f32[512,512]{1,0:T(8,128)}, u32[]{:S(2)}) copy-start(f32[512,512]{1,0:T(8,128)} %all-gather.5.cloned.1.call-done) | copy-start | bytes 3145732
Sparse Core Ops, SparseCore 0:
  14.9 206.1 reduce-scatter.1
  223.5 83.8 all-gather.4
  309.7 86.9 all-gather.6
where the time goes:
time: 537 us
  waiting for transfers between devices  378 us (70%)
  blocking collectives  125 us (23%)
  between operations  15.3 us (3%)
  matrix products  10.7 us (2%)
    reduce_scatter x1, waiting for transfers between devices, per_device(): lax.psum_scatter(gradient_rows(by_owner, activations), ('dp', 'seq'), sca...  206 us
    all_gather x1, waiting for transfers between devices, per_device(): lax.all_gather(right_root[0], ('seq', 'tensor'), axis=0, tiled=True)  87.3 us
    all_gather x1, waiting for transfers between devices, per_device(): slab_rows = lax.all_gather(grad_slab, ('seq', 'tensor'), axis=0, tiled=True)  83.4 us
    psum x1, blocking collectives, per_device(): adam_total = lax.psum(adam_part, ('seq', 'tensor'))  69.5 us
    all_gather x1, blocking collectives, per_device(): gathered = lax.all_gather(update_rows[None], 'dp', axis=0, tiled=True)  55.5 us
  transfers between devices with their start and end apart: 3, of which 3 were waited for; matrix products, arithmetic and copies ran while one was open for 1% of the time, Pallas kernels for 0%

commit v1 on v0

--- a/solution.py
+++ b/solution.py
@@ -59,7 +59,9 @@
     precond_total = lax.psum(precond_part, ("seq", "tensor"))
     graft_scale = jnp.sqrt(adam_total) / (jnp.sqrt(precond_total) + 1e-06)
     update_rows = (graft_scale * precond).astype(jnp.bfloat16)
-    gathered = lax.all_gather(update_rows[None], "dp", axis=0, tiled=True)
+    part = update_rows[None]
+    sent = jnp.stack([part] * lax.axis_size("dp"))
+    gathered = jnp.concatenate(lax.all_to_all(sent, "dp", 0, 0), axis=0)
     update = jnp.take(gathered, block_owner, axis=0)
     return (update, left_next[None], right_next[None], moment_next[None])
 

time: 537 us -> 504 us (0.939)
  the two profiles are of different devices: /device:TPU:2 before, /device:TPU:64 now
where the time goes in v1:
time: 504 us
  waiting for transfers between devices  385 us (76%)
  blocking collectives  72.7 us (14%)
  between operations  15.3 us (3%)
  matrix products  11.3 us (2%)
  starting transfers between devices  10.5 us (2%)
    reduce_scatter x1, waiting for transfers between devices, per_device(): lax.psum_scatter(gradient_rows(by_owner, activations), ('dp', 'seq'), sca...  204 us
    all_gather x1, waiting for transfers between devices, per_device(): lax.all_gather(right_root[0], ('seq', 'tensor'), axis=0, tiled=True)  87.3 us
    all_gather x1, waiting for transfers between devices, per_device(): slab_rows = lax.all_gather(grad_slab, ('seq', 'tensor'), axis=0, tiled=True)  84.6 us
    psum x1, blocking collectives, per_device(): adam_total = lax.psum(adam_part, ('seq', 'tensor'))  72.7 us
    all_to_all x1, starting transfers between devices, per_device(): gathered = jnp.concatenate(lax.all_to_all(sent, 'dp', 0, 0), axis=0)  10.3 us
  transfers between devices with their start and end apart: 4, of which 4 were waited for; matrix products, arithmetic and copies ran while one was open for 2% of the time, Pallas kernels for 0%

profile of v1, /device:TPU:64, one launch (start us, length us, event | category | flops | bytes accessed | tf_op | source)
XLA Modules:
  0.0 503.7 jit_solution(6059647440261891193)
XLA Ops:
  7.2 0.0 copy-start
  7.2 0.0 reduce-scatter.2.cloned.1.call-start
  7.2 0.8 select_reduce_fusion
  8.1 1.5 copy.18
  9.6 0.7 copy.19
  10.2 0.7 gather_fusion
  11.0 0.5 copy.20
  11.5 0.1 broadcast_bitcast_fusion
  11.6 0.5 bitcast_select_fusion
  12.1 0.0 copy-done
  12.1 2.6 fusion.11
  14.8 0.0 copy-start.7
  14.8 0.0 copy-start.3
  14.8 0.0 copy-start.4
  14.8 0.0 copy-start.5
  14.8 0.0 copy-start.6
  14.8 0.0 reduce-scatter.2.cloned.1.call-update
  14.8 0.0 all-gather.4.cloned.1.call-start
  14.9 204.5 %reduce-scatter.2.cloned.1.call-done = f32[16,512]{1,0:T(8,128)} async-done(((f32[2048,512]{1,0:T(8,128)}), f32[16,512]{1,0:T(8,128)}) %reduce-scatter.2.cloned.1.call-update) | async-done | bytes 32784 | tf_op jit(solution)/shard_map/reduce_scatter | solution.py:30
  219.3 0.0 copy-start.2
  219.3 0.0 all-gather.4.cloned.1.call-update
  219.4 0.0 all-gather.6.cloned.1.call-start
  219.4 0.7 all-gather.6.cloned.1.call-update
  220.1 0.0 copy-done.7
  220.1 0.0 copy-done.3
  220.1 2.0 fusion.8
  222.1 84.6 %all-gather.4.cloned.1.call-done = f32[512,512]{1,0:T(8,128)} async-done(((f32[16,512]{1,0:T(8,128)}), f32[512,512]{1,0:T(8,128)}) %all-gather.4.cloned.1.call-update) | async-done | bytes 1048592 | tf_op jit(solution)/shard_map/all_gather | solution.py:39
  306.7 0.0 copy-done.4
  306.7 0.0 copy-start.1
  306.7 2.0 fusion.6
  308.6 87.3 %all-gather.6.cloned.1.call-done = f32[1,512,512]{2,1,0:T(8,128)} async-done(((f32[1,16,512]{2,1,0:T(8,128)}), f32[1,512,512]{2,1,0:T(8,128)}) %all-gather.6.cloned.1.call-update) | async-done | bytes 1048592 | tf_op jit(solution)/shard_map/all_gather | solution.py:54
  395.9 2.4 multiply_reduce_fusion
  398.4 72.7 %all-reduce = (f32[]{:T(128)}, f32[]{:T(128)}) all-reduce(f32[]{:T(128)} %get-tuple-element.7, f32[]{:T(128)} %get-tuple-element.8), channel_id=1, replica_groups=mesh['dp'=16,'seq'=8,'tensor'=4] {'seq','tensor'}, use_global_device_ids=true, to_apply=%region_3.4 | all-reduce | flops 2 | bytes 16 | tf_op jit(solution)/shard_map/psum | solution.py:36
  472.5 0.7 stack.3
  473.3 10.3 %all-to-all-start = ((bf16[16,1,16,512]{3,2,1,0:T(8,128)(2,1)}), bf16[16,1,16,512]{3,2,1,0:T(8,128)(2,1)S(1)}, u32[]{:S(2)}, u32[]{:S(2)}) async-start(bf16[16,1,16,512]{3,2,1,0:T(8,128)(2,1)} %stack.3), calls=%async_computation.1 | async-start | bytes 524288 | tf_op jit(solution)/shard_map/all_to_all | solution.py:64
  483.6 0.0 copy-done.5
  483.6 2.6 fusion.1
  486.3 0.0 copy-done.6
  486.3 0.0 copy-done.2
  486.3 0.0 copy-done.1
  486.3 1.6 fusion
  487.9 7.9 %all-to-all-done = bf16[16,1,16,512]{3,2,1,0:T(8,128)(2,1)S(1)} async-done(((bf16[16,1,16,512]{3,2,1,0:T(8,128)(2,1)}), bf16[16,1,16,512]{3,2,1,0:T(8,128)(2,1)S(1)}, u32[]{:S(2)}, u32[]{:S(2)}) %all-to-all-start) | async-done | bytes 262176 | tf_op jit(solution)/shard_map/all_to_all | solution.py:64
  495.8 0.6 gather_fusion.1
  496.3 0.8 broadcast_select_fusion
  (7 shorter events, 0.0 us)
Async XLA Ops:
  7.2 5.0 copy-start
  7.2 212.1 %reduce-scatter.2.cloned.1.call-start = ((), (), s32[]{:S(2)}) async-start(), calls=%async_computation.2 | async-start | bytes 4227072 | tf_op jit(solution)/shard_map/reduce_scatter | solution.py:30
  14.8 205.3 %copy-start.7 = (s32[16]{0:T(128)S(1)}, s32[16]{0:T(128)}, u32[]{:S(2)}) copy-start(s32[16]{0:T(128)} %param.10) | copy-start | bytes 196
  14.8 205.4 %copy-start.3 = (f32[1,16,512]{2,1,0:T(8,128)S(1)}, f32[1,16,512]{2,1,0:T(8,128)}, u32[]{:S(2)}) copy-start(f32[1,16,512]{2,1,0:T(8,128)} %param.13) | copy-start | bytes 98308
  14.8 291.9 %copy-start.4 = (f32[1,16,512]{2,1,0:T(8,128)S(1)}, f32[1,16,512]{2,1,0:T(8,128)}, u32[]{:S(2)}) copy-start(f32[1,16,512]{2,1,0:T(8,128)} %param.14) | copy-start | bytes 98308
  14.8 468.8 %copy-start.5 = (f32[1,16,512]{2,1,0:T(8,128)S(1)}, f32[1,16,512]{2,1,0:T(8,128)}, u32[]{:S(2)}) copy-start(f32[1,16,512]{2,1,0:T(8,128)} %param.12) | copy-start | bytes 98308
  14.8 471.5 %copy-start.6 = (f32[1,16,512]{2,1,0:T(8,128)S(1)}, f32[1,16,512]{2,1,0:T(8,128)}, u32[]{:S(2)}) copy-start(f32[1,16,512]{2,1,0:T(8,128)} %param.11) | copy-start | bytes 98308
  14.8 291.9 %all-gather.4.cloned.1.call-start = ((), (), s32[]{:S(2)}) async-start(), calls=%async_computation.3 | async-start | bytes 1081344 | tf_op jit(solution)/shard_map/all_gather | solution.py:39
  219.3 266.9 %copy-start.2 = (f32[16,512]{1,0:T(8,128)S(1)}, f32[16,512]{1,0:T(8,128)}, u32[]{:S(2)}) copy-start(f32[16,512]{1,0:T(8,128)} %reduce-scatter.2.cloned.1.call-done) | copy-start | bytes 98308
  219.4 176.6 %all-gather.6.cloned.1.call-start = ((), (), s32[]{:S(2)}) async-start(), calls=%async_computation.4 | async-start | bytes 1081344 | tf_op jit(solution)/shard_map/all_gather | solution.py:54
  306.7 179.6 %copy-start.1 = (f32[512,512]{1,0:T(8,128)S(1)}, f32[512,512]{1,0:T(8,128)}, u32[]{:S(2)}) copy-start(f32[512,512]{1,0:T(8,128)} %all-gather.4.cloned.1.call-done) | copy-start | bytes 3145732
  473.3 22.5 %all-to-all-start = ((bf16[16,1,16,512]{3,2,1,0:T(8,128)(2,1)}), bf16[16,1,16,512]{3,2,1,0:T(8,128)(2,1)S(1)}, u32[]{:S(2)}, u32[]{:S(2)}) async-start(bf16[16,1,16,512]{3,2,1,0:T(8,128)(2,1)} %stack.3), calls=%async_computation.1 | async-start | bytes 524288 | tf_op jit(solution)/shard_map/all_to_all | solution.py:64
Sparse Core Ops, SparseCore 0:
  14.9 204.3 reduce-scatter.1
  221.6 84.9 all-gather.3
  309.0 86.9 all-gather.5
